TPU v7x, 32 devices: a whole 2x2x4 slice. The times are simulated.
32 devices in a mesh: groups: 2 (over y), ctx: 16 (over z, x, core).
Axes of the slice: x: 2, y: 2, z: 4, core: 2. Of those that a mesh axis runs over, the one named last changes fastest.
Arguments:
- inputs: bfloat16 [4096, 1536], P(('groups', 'ctx')), parts along dimension 0, may hold values from -6 to 6
- cotangent: bfloat16 [4096, 1536], P(('groups', 'ctx')), parts along dimension 0, may hold values from -6 to 6
- w_taps: bfloat16 [4608, 384], replicated, may hold values from -0.09375 to 0.09375
- w_out: bfloat16 [384, 1536], replicated, may hold values from -0.3125 to 0.3125
Outputs:
- outputs: bfloat16 [4096, 1536], P(('groups', 'ctx')), parts along dimension 0
- grad_input: bfloat16 [4096, 1536], P(('groups', 'ctx')), parts along dimension 0
- grad_taps: float32 [9216, 384], P(('groups', 'ctx')), parts along dimension 0
There are 2 independent parts, one for each index of `groups`. A program takes and returns all parts, laid end to end along the dimension named above; an argument that names none is the same for every part. Nothing has to cross between parts.
All inputs are finite; a program needn't handle non-finite values.
Results may differ from a plain program's by a relative error of at most 0.0053.
Values may be sent and summed in bfloat16 or wider, within the bound.
A program may use at most 64 MiB of HBM per device.

v0:
```python
import math

import jax
import jax.numpy as jnp
from jax import lax
from jax.sharding import PartitionSpec as P


def passed_along(array, axis, by):
    length = lax.axis_size(axis)
    pairs = [(i, i + by) for i in range(length) if 0 <= i + by < length]
    return lax.ppermute(array, axis, pairs)


def normalize(values):
    centre = jnp.mean(values, axis=1, keepdims=True)
    spread = jnp.mean(jnp.square(values - centre), axis=1, keepdims=True)
    return jax.nn.gelu((values - centre) * lax.rsqrt(spread + 1e-05))


def body(inputs, cotangent, w_taps, w_out):
    hop_count = lax.axis_size("ctx") // 8
    bin_rows = inputs.shape[0]
    channels = inputs.shape[1]
    devices_ctx = lax.axis_size("ctx")
    grad_scale = 1.0 / math.sqrt(bin_rows * devices_ctx)
    as_float = inputs.astype(jnp.float32)
    acts_full, act_vjp = jax.vjp(normalize, as_float)
    activation_rows = acts_full.astype(jnp.bfloat16)
    acts_prior = passed_along(activation_rows, "ctx", hop_count)
    acts_next = passed_along(activation_rows, "ctx", -hop_count)
    stacked_taps_input = jnp.concatenate([acts_prior, activation_rows, acts_next], axis=1)
    hidden = jnp.dot(stacked_taps_input, w_taps, preferred_element_type=jnp.float32)
    gated_full, gelu_vjp = jax.vjp(jax.nn.gelu, hidden)
    gated = gated_full.astype(jnp.bfloat16)
    outputs = (as_float + jnp.dot(gated, w_out, preferred_element_type=jnp.float32)).astype(
        jnp.bfloat16
    )
    back = lax.dot_general(
        cotangent, w_out, (((1,), (1,)), ((), ())), preferred_element_type=jnp.float32
    )
    dhid = gelu_vjp(back)[0].astype(jnp.bfloat16)
    grad_taps = lax.psum_scatter(
        lax.dot_general(
            stacked_taps_input, dhid, (((0,), (0,)), ((), ())), preferred_element_type=jnp.float32
        )
        * grad_scale,
        "ctx",
        scatter_dimension=0,
        tiled=True,
    )
    tap_products = lax.dot_general(
        dhid, w_taps, (((1,), (1,)), ((), ())), preferred_element_type=jnp.float32
    )
    from_next = passed_along(
        tap_products[:, :channels].astype(jnp.bfloat16), "ctx", -hop_count
    ).astype(jnp.float32)
    from_prior = passed_along(
        tap_products[:, 2 * channels :].astype(jnp.bfloat16), "ctx", hop_count
    ).astype(jnp.float32)
    activation_gradient = from_next + tap_products[:, channels : 2 * channels] + from_prior
    grad_input = (cotangent.astype(jnp.float32) + act_vjp(activation_gradient)[0]).astype(
        jnp.bfloat16
    )
    return (outputs, grad_input, grad_taps)


def solution(mesh):
    return jax.shard_map(
        body,
        mesh=mesh,
        in_specs=(P(("groups", "ctx"), None), P(("groups", "ctx"), None), P(), P()),
        out_specs=(
            P(("groups", "ctx"), None),
            P(("groups", "ctx"), None),
            P(("groups", "ctx"), None),
        ),
        check_vma=False,
    )
```

profile of v0, /device:TPU:17, one launch (start us, length us, event | category | flops | bytes accessed | tf_op | source)
XLA Modules:
  0.0 136.3 jit_solution(14331519789001579484)
XLA Ops:
  7.2 0.0 copy-start
  7.2 0.0 reduce-scatter.2.cloned.1.call-start
  7.2 1.3 convert_reduce_fusion
  8.5 1.2 fusion.24
  9.8 1.5 %fusion.21 = bf16[128,1536]{1,0:T(8,128)(2,1)S(1)} fusion(bf16[128,1536]{1,0:T(8,128)(2,1)} %param.4, f32[128]{0:T(128)S(1)} %fusion.39, f32[128]{0:T(128)S(1)} %broadcast_multiply_fusion), kind=kLoop, calls=%fused_computation.26 | loop fusion | flops 2359296 | bytes 787456 | tf_op jit(solution)/shard_map/convert_element_type | solution.py:29
  11.3 3.1 %collective-permute-start = (bf16[128,1536]{1,0:T(8,128)(2,1)S(1)}, bf16[128,1536]{1,0:T(8,128)(2,1)S(1)}, u32[]{:S(2)}, u32[]{:S(2)}) collective-permute-start(bf16[128,1536]{1,0:T(8,128)(2,1)S(1)} %fusion.21), channel_id=1, source_target_pairs={{0,2},{1,3},{2,4},{3,5},{4,6},{5,7},{6,8},{7,9},{8,10},{9,11},{10,... | collective-permute-start | bytes 1179656 | tf_op jit(solution)/shard_map/ppermute | solution.py:12
  14.4 3.1 %collective-permute-start.1 = (bf16[128,1536]{1,0:T(8,128)(2,1)S(1)}, bf16[128,1536]{1,0:T(8,128)(2,1)S(1)}, u32[]{:S(2)}, u32[]{:S(2)}) collective-permute-start(bf16[128,1536]{1,0:T(8,128)(2,1)S(1)} %fusion.21), channel_id=1, source_target_pairs={{2,0},{3,1},{4,2},{5,3},{6,4},{7,5},{8,6},{9,7},{10,8},{11,9},{12,... | collective-permute-start | bytes 1179656 | tf_op jit(solution)/shard_map/ppermute | solution.py:12
  17.5 1.9 %fusion.49 = f32[128,384]{1,0:T(8,128)S(1)} fusion(bf16[128,1536]{1,0:T(8,128)(2,1)} %param.5, bf16[384,1536]{1,0:T(8,128)(2,1)} %param.7), kind=kOutput, calls=%fused_computation.62 | convolution fusion | flops 150994944 | bytes 1769472 | tf_op jit(solution)/shard_map/dot_general | solution.py:39
  19.4 11.2 %collective-permute-done = bf16[128,1536]{1,0:T(8,128)(2,1)S(1)} collective-permute-done((bf16[128,1536]{1,0:T(8,128)(2,1)S(1)}, bf16[128,1536]{1,0:T(8,128)(2,1)S(1)}, u32[]{:S(2)}, u32[]{:S(2)}) %collective-permute-start) | collective-permute-done | bytes 393248 | tf_op jit(solution)/shard_map/ppermute | solution.py:12
  30.6 2.9 %collective-permute-done.1 = bf16[128,1536]{1,0:T(8,128)(2,1)S(1)} collective-permute-done((bf16[128,1536]{1,0:T(8,128)(2,1)S(1)}, bf16[128,1536]{1,0:T(8,128)(2,1)S(1)}, u32[]{:S(2)}, u32[]{:S(2)}) %collective-permute-start.1) | collective-permute-done | bytes 393248 | tf_op jit(solution)/shard_map/ppermute | solution.py:12
  33.5 0.0 copy-done
  33.5 1.5 %fusion.34 = (bf16[128,384]{1,0:T(8,128)(2,1)S(1)}, f32[128,384]{1,0:T(8,128)}) fusion(f32[128,384]{1,0:T(8,128)S(1)} %fusion.49, bf16[4608,384]{1,0:T(8,128)(2,1)S(1)} %copy-done, bf16[128,1536]{1,0:T(8,128)(2,1)S(1)} %collective-permute-done.1, bf16[128,1536]{1,0:T(8,128)(2,1)S(1)} %fusion.21, bf16[128,1536]{1,0:T(8,128)(2,1)S(1)} %collective-permute-done), kind=kOutput, calls=%fused_computation.43 | convolution fusion | flops 457506816 | bytes 5210112 | tf_op jit(solution)/shard_map/dot_general | solution.py:33
  35.1 0.0 copy-start.4
  35.1 0.6 copy-done.4
  35.7 4.0 %convolution_multiply_fusion = f32[4608,384]{1,0:T(8,128)} fusion(bf16[128,384]{1,0:T(8,128)(2,1)S(1)} %get-tuple-element.8, bf16[128,1536]{1,0:T(8,128)(2,1)S(1)} %collective-permute-done.1, bf16[128,1536]{1,0:T(8,128)(2,1)S(1)} %fusion.21, bf16[128,1536]{1,0:T(8,128)(2,1)S(1)} %collective-permute-done), kind=kOutput, calls=%fused_computation | convolution fusion | flops 458293248 | bytes 8355840 | tf_op jit(solution)/shard_map/dot_general | solution.py:44
  39.7 0.0 reduce-scatter.2.cloned.1.call-update
  39.7 0.0 copy-start.1
  39.8 0.0 copy-start.2
  39.8 0.0 copy-start.5
  39.8 2.2 %fusion.48 = (bf16[128,4608]{1,0:T(8,128)(2,1)S(1)}, f32[128,4608]{1,0:T(8,128)S(1)}) fusion(bf16[128,384]{1,0:T(8,128)(2,1)} %copy-done.4, bf16[4608,384]{1,0:T(8,128)(2,1)S(1)} %copy-done), kind=kOutput, calls=%fused_computation.61 | convolution fusion | flops 453574656 | bytes 7176192 | tf_op jit(solution)/shard_map/dot_general | solution.py:52
  42.0 0.1 fusion.47
  42.1 1.9 %collective-permute-start.2 = (bf16[128,1536]{1,0:T(8,128)(2,1)S(1)}, bf16[128,1536]{1,0:T(8,128)(2,1)S(1)}, u32[]{:S(2)}, u32[]{:S(2)}) collective-permute-start(bf16[128,1536]{1,0:T(8,128)(2,1)S(1)} %get-tuple-element.6), channel_id=1, source_target_pairs={{2,0},{3,1},{4,2},{5,3},{6,4},{7,5},{8,6},{9,7},{10,8},{11,9},{12,... | collective-permute-start | bytes 1179656 | tf_op jit(solution)/shard_map/ppermute | solution.py:12
  44.0 3.4 %collective-permute-start.3 = (bf16[128,1536]{1,0:T(8,128)(2,1)S(1)}, bf16[128,1536]{1,0:T(8,128)(2,1)S(1)}, u32[]{:S(2)}, u32[]{:S(2)}) collective-permute-start(bf16[128,1536]{1,0:T(8,128)(2,1)S(1)} %get-tuple-element.7), channel_id=1, source_target_pairs={{0,2},{1,3},{2,4},{3,5},{4,6},{5,7},{6,8},{7,9},{8,10},{9,11},{10,... | collective-permute-start | bytes 1179656 | tf_op jit(solution)/shard_map/ppermute | solution.py:12
  47.4 0.0 copy-done.1
  47.4 0.0 copy-done.2
  47.4 0.0 copy-done.5
  47.4 0.0 copy-start.3
  47.4 1.1 fusion
  48.6 14.0 %collective-permute-done.2 = bf16[128,1536]{1,0:T(8,128)(2,1)S(1)} collective-permute-done((bf16[128,1536]{1,0:T(8,128)(2,1)S(1)}, bf16[128,1536]{1,0:T(8,128)(2,1)S(1)}, u32[]{:S(2)}, u32[]{:S(2)}) %collective-permute-start.2) | collective-permute-done | bytes 393248 | tf_op jit(solution)/shard_map/ppermute | solution.py:12
  62.6 0.0 collective-permute-done.3
  62.6 0.9 multiply_reduce_fusion
  63.5 0.3 fusion.11
  63.8 0.0 copy-done.3
  63.8 1.0 fusion.15
  64.9 64.6 %reduce-scatter.2.cloned.1.call-done = f32[288,384]{1,0:T(8,128)} async-done(((f32[4608,384]{1,0:T(8,128)}), f32[288,384]{1,0:T(8,128)}) %reduce-scatter.2.cloned.1.call-update) | async-done | bytes 442384 | tf_op jit(solution)/shard_map/reduce_scatter | solution.py:43
  (4 shorter events, 0.0 us)
Async XLA Ops:
  7.2 26.4 %copy-start = (bf16[4608,384]{1,0:T(8,128)(2,1)S(1)}, bf16[4608,384]{1,0:T(8,128)(2,1)}, u32[]{:S(2)}) copy-start(bf16[4608,384]{1,0:T(8,128)(2,1)} %param.6) | copy-start | bytes 10616836
  7.2 122.3 %reduce-scatter.2.cloned.1.call-start = ((), (), s32[]{:S(2)}) async-start(), calls=%async_computation.1 | async-start | bytes 7520256 | tf_op jit(solution)/shard_map/reduce_scatter | solution.py:43
  11.3 19.3 %collective-permute-start = (bf16[128,1536]{1,0:T(8,128)(2,1)S(1)}, bf16[128,1536]{1,0:T(8,128)(2,1)S(1)}, u32[]{:S(2)}, u32[]{:S(2)}) collective-permute-start(bf16[128,1536]{1,0:T(8,128)(2,1)S(1)} %fusion.21), channel_id=1, source_target_pairs={{0,2},{1,3},{2,4},{3,5},{4,6},{5,7},{6,8},{7,9},{8,10},{9,11},{10,... | collective-permute-start | bytes 1179656 | tf_op jit(solution)/shard_map/ppermute | solution.py:12
  14.4 19.1 %collective-permute-start.1 = (bf16[128,1536]{1,0:T(8,128)(2,1)S(1)}, bf16[128,1536]{1,0:T(8,128)(2,1)S(1)}, u32[]{:S(2)}, u32[]{:S(2)}) collective-permute-start(bf16[128,1536]{1,0:T(8,128)(2,1)S(1)} %fusion.21), channel_id=1, source_target_pairs={{2,0},{3,1},{4,2},{5,3},{6,4},{7,5},{8,6},{9,7},{10,8},{11,9},{12,... | collective-permute-start | bytes 1179656 | tf_op jit(solution)/shard_map/ppermute | solution.py:12
  35.1 0.6 copy-start.4
  39.7 7.6 %copy-start.1 = (bf16[128,1536]{1,0:T(8,128)(2,1)S(1)}, bf16[128,1536]{1,0:T(8,128)(2,1)}, u32[]{:S(2)}) copy-start(bf16[128,1536]{1,0:T(8,128)(2,1)} %param.4) | copy-start | bytes 1179652
  39.8 7.6 %copy-start.2 = (bf16[384,1536]{1,0:T(8,128)(2,1)S(1)}, bf16[384,1536]{1,0:T(8,128)(2,1)}, u32[]{:S(2)}) copy-start(bf16[384,1536]{1,0:T(8,128)(2,1)} %param.7) | copy-start | bytes 3538948
  39.8 7.6 %copy-start.5 = (f32[128,384]{1,0:T(8,128)S(1)}, f32[128,384]{1,0:T(8,128)}, u32[]{:S(2)}) copy-start(f32[128,384]{1,0:T(8,128)} %get-tuple-element.9) | copy-start | bytes 589828
  42.1 20.5 %collective-permute-start.2 = (bf16[128,1536]{1,0:T(8,128)(2,1)S(1)}, bf16[128,1536]{1,0:T(8,128)(2,1)S(1)}, u32[]{:S(2)}, u32[]{:S(2)}) collective-permute-start(bf16[128,1536]{1,0:T(8,128)(2,1)S(1)} %get-tuple-element.6), channel_id=1, source_target_pairs={{2,0},{3,1},{4,2},{5,3},{6,4},{7,5},{8,6},{9,7},{10,8},{11,9},{12,... | collective-permute-start | bytes 1179656 | tf_op jit(solution)/shard_map/ppermute | solution.py:12
  44.0 18.6 %collective-permute-start.3 = (bf16[128,1536]{1,0:T(8,128)(2,1)S(1)}, bf16[128,1536]{1,0:T(8,128)(2,1)S(1)}, u32[]{:S(2)}, u32[]{:S(2)}) collective-permute-start(bf16[128,1536]{1,0:T(8,128)(2,1)S(1)} %get-tuple-element.7), channel_id=1, source_target_pairs={{0,2},{1,3},{2,4},{3,5},{4,6},{5,7},{6,8},{7,9},{8,10},{9,11},{10,... | collective-permute-start | bytes 1179656 | tf_op jit(solution)/shard_map/ppermute | solution.py:12
  47.4 16.4 %copy-start.3 = (bf16[128,1536]{1,0:T(8,128)(2,1)S(1)}, bf16[128,1536]{1,0:T(8,128)(2,1)}, u32[]{:S(2)}) copy-start(bf16[128,1536]{1,0:T(8,128)(2,1)} %param.5) | copy-start | bytes 1179652
Sparse Core Ops, SparseCore 0:
  39.9 89.5 reduce-scatter.1
where the time goes:
time: 139 us; the launch traced here: 136 us
  waiting for transfers between devices  92.8 us (67%)
  between operations  14.2 us (10%)
  starting transfers between devices  11.5 us (8%)
  matrix products  10.8 us (8%)
  other arithmetic  6.29 us (5%)
    reduce_scatter x1, waiting for transfers between devices, body(): lax.psum_scatter(lax.dot_general(stacked_taps_input, dhid, (((0,), (0,)),...  64.6 us
    ppermute x4, waiting for transfers between devices, passed_along(): return lax.ppermute(array, axis, pairs)  28.2 us
    ppermute x4, starting transfers between devices, passed_along(): return lax.ppermute(array, axis, pairs)  11.5 us
    dot_general x1, matrix products, body(): lax.dot_general(stacked_taps_input, dhid, (((0,), (0,)), ((), ())), prefe...  4.02 us
  transfers between devices with their start and end apart: 5, of which 4 were waited for; matrix products, arithmetic and copies ran while one was open for 6% of the time, Pallas kernels for 0%

commit v1 on v0

v1 whole, which is shorter than its diff:
```python
import functools
import math

import jax
import jax.numpy as jnp
from jax import lax
from jax.experimental import pallas as pl
from jax.experimental.pallas import tpu as pltpu
from jax.sharding import PartitionSpec as P

F32 = jnp.float32
BF16 = jnp.bfloat16
C0 = math.sqrt(2.0 / math.pi)
C1 = 0.044715
CHUNK = 16
SUB = 96


def nt_dot(a, b):
    return lax.dot_general(a, b, (((1,), (1,)), ((), ())), preferred_element_type=F32)


def gelu_pair(v):
    sq = v * v
    t = jnp.tanh(v * (C0 + (C0 * C1) * sq))
    half = 0.5 + 0.5 * t
    value = v * half
    slope = half + (0.5 * v) * (1.0 - t * t) * (C0 + (3.0 * C0 * C1) * sq)
    return value, slope


def fused(
    scale, x_ref, ct_ref, wt_hbm, wo_hbm, out_ref, gi_ref, gt_ref,
    wt, wo, acts, acts_t, v_buf, slope_buf, r_buf, blocks, dh, h_send, h_recv, p_send, p_recv,
    w_sem, hs_sem, hr_sem, as_sem, ar_sem, ds_sem, dr_sem, es_sem, ps_sem, pr_sem,
):
    me = lax.axis_index("ctx")
    rows, channels = x_ref.shape
    own_rows = gt_ref.shape[0]
    half = me // 8
    base = half * 8
    place = me - base
    core = me % 2
    pair = place // 2
    mirror = (me + 8) % 16

    def to(index):
        return {"ctx": index}

    def remote(src, dst, send, recv, index):
        return pltpu.make_async_remote_copy(
            src_ref=src, dst_ref=dst, send_sem=send, recv_sem=recv,
            device_id=to(index), device_id_type=pl.DeviceIdType.MESH,
        )

    w_copies = [
        pltpu.make_async_copy(wt_hbm.at[pl.ds(k * channels, channels)],
                              wt.at[pl.ds(k * channels, channels)], w_sem.at[n])
        for n, k in enumerate((0, 2, 1))
    ]
    w_copies.append(pltpu.make_async_copy(wo_hbm, wo, w_sem.at[3]))
    for copy in w_copies:
        copy.start()

    barrier = pltpu.get_barrier_semaphore()
    for i in range(1, 16):
        pl.semaphore_signal(barrier, inc=1, device_id=to((me + i) % 16),
                            device_id_type=pl.DeviceIdType.MESH)

    for n in range(rows // CHUNK):
        part = pl.ds(n * CHUNK, CHUNK)
        x = x_ref[part, :].astype(F32)
        mu = jnp.mean(x, axis=1, keepdims=True)
        xc = x - mu
        r = lax.rsqrt(jnp.mean(xc * xc, axis=1, keepdims=True) + 1e-5)
        v = xc * r
        v_buf[part, :] = v
        r_buf[part, :] = jnp.broadcast_to(r, (CHUNK, 128))
        t = jnp.tanh(v * (C0 + (C0 * C1) * (v * v)))
        acts[part, :] = (v * (0.5 + 0.5 * t)).astype(BF16)

    w_copies[0].wait()
    h_send[0] = jnp.dot(acts[...], wt[0:channels, :], preferred_element_type=F32).astype(BF16)
    w_copies[1].wait()
    h_send[1] = jnp.dot(acts[...], wt[2 * channels:, :], preferred_element_type=F32).astype(BF16)
    pl.semaphore_wait(barrier, 15)

    h_up = remote(h_send.at[0], h_recv.at[0], hs_sem.at[0], hr_sem.at[0], jnp.minimum(me + 2, 15))
    h_down = remote(h_send.at[1], h_recv.at[1], hs_sem.at[1], hr_sem.at[1], jnp.maximum(me - 2, 0))

    @pl.when(me < 14)
    def _():
        h_up.start()

    @pl.when(me >= 2)
    def _():
        h_down.start()

    @pl.when(me < 2)
    def _():
        h_recv[0] = jnp.zeros(h_recv.shape[1:], BF16)

    @pl.when(me >= 14)
    def _():
        h_recv[1] = jnp.zeros(h_recv.shape[1:], BF16)

    acts_t[0:channels, :] = acts[...].astype(F32).T.astype(BF16)
    acts_t[channels:, :] = acts_t[0:own_rows, :]

    def block_of(target):
        return acts_t.at[pl.ds(pl.multiple_of((target * own_rows) % channels, SUB), own_rows)]

    a_copies = []
    for i in range(1, 8):
        peer = base + (place + i) % 8
        for b in range(2):
            copy = remote(block_of((peer + 8 * b) % 16), blocks.at[place, b],
                          as_sem.at[i, b], ar_sem.at[place, b], peer)
            copy.start()
            a_copies.append(copy)
    for b in range(2):
        blocks[place, b] = block_of((me + 8 * b) % 16)[...]

    dh[5 * half] = jnp.zeros(dh.shape[1:], BF16)

    w_copies[2].wait()
    h_mid = jnp.dot(acts[...], wt[channels:2 * channels, :], preferred_element_type=F32)
    w_copies[3].wait()
    back = nt_dot(ct_ref[...], wo[...])
    for n in range(rows // CHUNK):
        part = pl.ds(n * CHUNK, CHUNK)
        slope_buf[part, :] = gelu_pair(v_buf[part, :])[1]

    @pl.when(me >= 2)
    def _():
        h_up.wait_recv()

    @pl.when(me < 14)
    def _():
        h_down.wait_recv()

    hidden = h_mid + h_recv[0].astype(F32) + h_recv[1].astype(F32)
    gated, slope = gelu_pair(hidden)
    gated = gated.astype(BF16)
    mine = dh.at[1 + pair, pl.ds(pl.multiple_of(core * rows, rows), rows)]
    mine[...] = (back * slope).astype(BF16)

    spot = 2 * (1 + pair) + core
    d_copies = []
    for i in (2, 6, 1, 3, 7, 5, 4):
        peer = base + (place + i) % 8
        copy = remote(mine, mine, ds_sem.at[i], dr_sem.at[spot], peer)
        copy.start()
        d_copies.append(copy)

    edge_slot = 5 * half
    far = base + 8 - 16 * half
    at_edge = (me >= 6) & (me < 10)
    e_copies = [
        remote(mine, dh.at[edge_slot, pl.ds(pl.multiple_of(core * rows, rows), rows)],
               es_sem.at[i], dr_sem.at[2 * edge_slot + core], far + i)
        for i in range(8)
    ]

    @pl.when(at_edge)
    def _():
        for copy in e_copies:
            copy.start()

    out_ref[...] = (x_ref[...].astype(F32)
                    + jnp.dot(gated, wo[...], preferred_element_type=F32)).astype(BF16)

    def wait_slot(slot):
        remote(mine, mine, ds_sem.at[0], dr_sem.at[slot], mirror).wait_recv()

    lower, upper = spot - 2, spot + 2
    unused = 10 * half
    for slot in (lower, upper):
        @pl.when(slot // 2 != unused // 2)
        def _(slot=slot):
            wait_slot(slot)

    def core_rows(index):
        return dh[index, pl.ds(pl.multiple_of(core * rows, rows), rows), :]

    d_next, d_mid, d_prior = core_rows(pair + 2), core_rows(pair + 1), core_rows(pair)
    d_acts = nt_dot(d_next, wt[0:channels, :])
    d_acts = d_acts + nt_dot(d_mid, wt[channels:2 * channels, :])
    slope_buf[...] = (d_acts + nt_dot(d_prior, wt[2 * channels:, :])) * slope_buf[...]
    for n in range(rows // CHUNK):
        part = pl.ds(n * CHUNK, CHUNK)
        dv = slope_buf[part, :]
        v = v_buf[part, :]
        first = jnp.mean(dv, axis=1, keepdims=True)
        second = jnp.mean(dv * v, axis=1, keepdims=True)
        gi_ref[part, :] = (ct_ref[part, :].astype(F32)
                           + r_buf[part, 0:1] * (dv - first - v * second)).astype(BF16)

    for slot in range(12):
        @pl.when((slot != spot) & (slot != lower) & (slot != upper) & (slot // 2 != unused // 2))
        def _(slot=slot):
            wait_slot(slot)
    for i in range(1, 8):
        slot = (place + i) % 8
        for b in range(2):
            remote(blocks.at[slot, b], blocks.at[slot, b], as_sem.at[0, b],
                   ar_sem.at[slot, b], mirror).wait_recv()

    def term(b, j):
        tap = (3 * ((me + 8 * b) % 16) + j) // 16
        left = jnp.concatenate([blocks[s, b, j * SUB:(j + 1) * SUB, :] for s in range(8)], axis=1)
        right = dh[pl.ds(2 - tap, 4)].reshape(8 * rows, dh.shape[2])
        return jnp.dot(left, right, preferred_element_type=F32)

    for j in range(3):
        p_send[j * SUB:(j + 1) * SUB, :] = term(1, j).astype(BF16)
    p_copy = remote(p_send, p_recv, ps_sem, pr_sem, mirror)
    p_copy.start()
    for j in range(3):
        gt_ref[j * SUB:(j + 1) * SUB, :] = term(0, j)
    p_copy.wait_recv()
    gt_ref[...] = (gt_ref[...] + p_recv[...].astype(F32)) * scale

    @pl.when(me < 14)
    def _():
        h_up.wait_send()

    @pl.when(me >= 2)
    def _():
        h_down.wait_send()

    @pl.when(at_edge)
    def _():
        for copy in e_copies:
            copy.wait_send()

    for copy in a_copies + d_copies:
        copy.wait_send()
    p_copy.wait_send()


def fused_body(inputs, cotangent, w_taps, w_out):
    rows, channels = inputs.shape
    inner = w_taps.shape[1]
    count = lax.axis_size("ctx")
    own_rows = w_taps.shape[0] // count
    scale = 1.0 / math.sqrt(rows * count)
    vmem = pl.BlockSpec(memory_space=pltpu.VMEM)
    hbm = pl.BlockSpec(memory_space=pl.ANY)
    dma = pltpu.SemaphoreType.DMA
    return pl.pallas_call(
        functools.partial(fused, scale),
        out_shape=(
            jax.ShapeDtypeStruct((rows, channels), BF16),
            jax.ShapeDtypeStruct((rows, channels), BF16),
            jax.ShapeDtypeStruct((own_rows, inner), F32),
        ),
        in_specs=[vmem, vmem, hbm, hbm],
        out_specs=(vmem, vmem, vmem),
        scratch_shapes=[
            pltpu.VMEM(w_taps.shape, BF16),
            pltpu.VMEM(w_out.shape, BF16),
            pltpu.VMEM((rows, channels), BF16),
            pltpu.VMEM((channels + own_rows, rows), BF16),
            pltpu.VMEM((rows, channels), F32),
            pltpu.VMEM((rows, channels), F32),
            pltpu.VMEM((rows, 128), F32),
            pltpu.VMEM((8, 2, own_rows, rows), BF16),
            pltpu.VMEM((6, 2 * rows, inner), BF16),
            pltpu.VMEM((2, rows, inner), BF16),
            pltpu.VMEM((2, rows, inner), BF16),
            pltpu.VMEM((own_rows, inner), BF16),
            pltpu.VMEM((own_rows, inner), BF16),
            dma((4,)),
            dma((2,)),
            dma((2,)),
            dma((8, 2)),
            dma((8, 2)),
            dma((8,)),
            dma((12,)),
            dma((8,)),
            dma,
            dma,
        ],
        compiler_params=pltpu.CompilerParams(
            collective_id=0, has_side_effects=True, vmem_limit_bytes=48 * 1024 * 1024
        ),
    )(inputs, cotangent, w_taps, w_out)


def passed_along(array, axis, by):
    length = lax.axis_size(axis)
    pairs = [(i, i + by) for i in range(length) if 0 <= i + by < length]
    return lax.ppermute(array, axis, pairs)


def normalize(values):
    centre = jnp.mean(values, axis=1, keepdims=True)
    spread = jnp.mean(jnp.square(values - centre), axis=1, keepdims=True)
    return jax.nn.gelu((values - centre) * lax.rsqrt(spread + 1e-05))


def plain_body(inputs, cotangent, w_taps, w_out):
    hop = lax.axis_size("ctx") // 8
    rows, channels = inputs.shape
    scale = 1.0 / math.sqrt(rows * lax.axis_size("ctx"))
    w0, w1, w2 = (w_taps[k * channels:(k + 1) * channels] for k in range(3))
    as_float = inputs.astype(F32)
    acts_full, act_vjp = jax.vjp(normalize, as_float)
    acts = acts_full.astype(BF16)
    hidden = jnp.dot(acts, w1, preferred_element_type=F32)
    hidden += passed_along(jnp.dot(acts, w0, preferred_element_type=F32), "ctx", hop)
    hidden += passed_along(jnp.dot(acts, w2, preferred_element_type=F32), "ctx", -hop)
    gated_full, gelu_vjp = jax.vjp(jax.nn.gelu, hidden)
    outputs = (as_float + jnp.dot(gated_full.astype(BF16), w_out,
                                  preferred_element_type=F32)).astype(BF16)
    back = nt_dot(cotangent, w_out)
    dhid = gelu_vjp(back)[0].astype(BF16)
    d_next = passed_along(dhid, "ctx", -hop)
    d_prior = passed_along(dhid, "ctx", hop)
    terms = [
        lax.dot_general(acts, d, (((0,), (0,)), ((), ())), preferred_element_type=F32)
        for d in (d_next, dhid, d_prior)
    ]
    grad_taps = lax.psum_scatter(jnp.concatenate(terms, axis=0) * scale, "ctx",
                                 scatter_dimension=0, tiled=True)
    d_acts = nt_dot(d_next, w0) + nt_dot(dhid, w1) + nt_dot(d_prior, w2)
    grad_input = (cotangent.astype(F32) + act_vjp(d_acts)[0]).astype(BF16)
    return (outputs, grad_input, grad_taps)


def solution(mesh):
    spec = P(("groups", "ctx"), None)
    return jax.shard_map(
        fused_body if mesh.shape["ctx"] == 16 else plain_body,
        mesh=mesh,
        in_specs=(spec, spec, P(), P()),
        out_specs=(spec, spec, spec),
        check_vma=False,
    )
```

time: 139 us -> 58.1 us (0.42)
  the two profiles are of different devices: /device:TPU:17 before, /device:TPU:30 now
where the time goes in v1:
time: 58.1 us; the launch traced here: 57.9 us
  Pallas kernels  51.7 us (89%)
  local copies, waits for them, and re-layouts  5.51 us (9%)
  between operations  0.65 us (1%)
    pallas_call x1, Pallas kernels, fused_body(): pl.pallas_call(functools.partial(fused, scale), out_shape=(jax.ShapeDtype...  51.7 us
    unnamed x9, local copies, waits for them, and re-layouts  5.51 us

profile of v1, /device:TPU:30, one launch (start us, length us, event | category | flops | bytes accessed | tf_op | source)
XLA Modules:
  0.0 57.9 jit_solution(14185385782021713044)
XLA Ops:
  0.6 0.0 copy-start
  0.6 1.3 %copy-done = bf16[384,1536]{1,0:T(8,128)(2,1)S(1)} copy-done((bf16[384,1536]{1,0:T(8,128)(2,1)S(1)}, bf16[384,1536]{1,0:T(8,128)(2,1)}, u32[]{:S(2)}) %copy-start) | copy-done | bytes 1179672
  1.9 0.0 copy-start.1
  1.9 1.0 %copy-done.1 = bf16[128,1536]{1,0:T(8,128)(2,1)S(1)} copy-done((bf16[128,1536]{1,0:T(8,128)(2,1)S(1)}, bf16[128,1536]{1,0:T(8,128)(2,1)}, u32[]{:S(2)}) %copy-start.1) | copy-done | bytes 393240
  2.9 0.0 copy-start.2
  2.9 1.0 %copy-done.2 = bf16[128,1536]{1,0:T(8,128)(2,1)S(1)} copy-done((bf16[128,1536]{1,0:T(8,128)(2,1)S(1)}, bf16[128,1536]{1,0:T(8,128)(2,1)}, u32[]{:S(2)}) %copy-start.2) | copy-done | bytes 393240
  3.9 51.7 %shard_map.67 = (bf16[128,1536]{1,0:T(8,128)(2,1)S(1)}, bf16[128,1536]{1,0:T(8,128)(2,1)S(1)}, f32[288,384]{1,0:T(8,128)S(1)}) custom-call(bf16[128,1536]{1,0:T(8,128)(2,1)S(1)} %copy-done.1, bf16[128,1536]{1,0:T(8,128)(2,1)S(1)} %copy-done.2, bf16[4608,384]{1,0:T(8,128)(2,1)} %wt_hbm.1, bf16[384,1536]{1,0:T(8,128)(2,1)S(1)} %copy-done), custom_call_target="tpu_custom_call" | custom-call | tf_op jit(solution)/shard_map/pallas_call | solution.py:251
  55.6 0.7 %copy.10 = bf16[128,1536]{1,0:T(8,128)(2,1)} copy(bf16[128,1536]{1,0:T(8,128)(2,1)S(1)} %get-tuple-element.6) | data formatting | bytes 786432
  56.4 0.7 %copy.11 = bf16[128,1536]{1,0:T(8,128)(2,1)} copy(bf16[128,1536]{1,0:T(8,128)(2,1)S(1)} %get-tuple-element.7) | data formatting | bytes 786432
  57.1 0.8 %copy.12 = f32[288,384]{1,0:T(8,128)} copy(f32[288,384]{1,0:T(8,128)S(1)} %get-tuple-element.8) | data formatting | bytes 884736
Async XLA Ops:
  0.6 1.3 %copy-start = (bf16[384,1536]{1,0:T(8,128)(2,1)S(1)}, bf16[384,1536]{1,0:T(8,128)(2,1)}, u32[]{:S(2)}) copy-start(bf16[384,1536]{1,0:T(8,128)(2,1)} %wo_hbm.1) | copy-start | bytes 3538948
  1.9 1.0 %copy-start.1 = (bf16[128,1536]{1,0:T(8,128)(2,1)S(1)}, bf16[128,1536]{1,0:T(8,128)(2,1)}, u32[]{:S(2)}) copy-start(bf16[128,1536]{1,0:T(8,128)(2,1)} %x_ref.1) | copy-start | bytes 1179652
  2.9 1.0 %copy-start.2 = (bf16[128,1536]{1,0:T(8,128)(2,1)S(1)}, bf16[128,1536]{1,0:T(8,128)(2,1)}, u32[]{:S(2)}) copy-start(bf16[128,1536]{1,0:T(8,128)(2,1)} %ct_ref.1) | copy-start | bytes 1179652

commit v2 on v1

--- a/solution.py
+++ b/solution.py
@@ -30,13 +30,13 @@
 
 
 def fused(
-    scale, x_ref, ct_ref, wt_hbm, wo_hbm, out_ref, gi_ref, gt_ref,
-    wt, wo, acts, acts_t, v_buf, slope_buf, r_buf, blocks, dh, h_send, h_recv, p_send, p_recv,
-    w_sem, hs_sem, hr_sem, as_sem, ar_sem, ds_sem, dr_sem, es_sem, ps_sem, pr_sem,
+    scale, x_hbm, ct_hbm, wt_hbm, wo_hbm, out_ref, gi_ref, gt_ref,
+    x_ref, ct_ref, wt, wo, acts, acts_t, v_buf, slope_buf, r_buf, blocks, dh, h_send, h_recv, p_send, p_recv,
+    w_sem, hs_sem, hr_sem, as_sem, ar_sem, ds_sem, dr_sem, es_sem, fs_sem, ps_sem, pr_sem,
 ):
     me = lax.axis_index("ctx")
     rows, channels = x_ref.shape
-    own_rows = gt_ref.shape[0]
+    width = channels // 8
     half = me // 8
     base = half * 8
     place = me - base
@@ -59,7 +59,9 @@
         for n, k in enumerate((0, 2, 1))
     ]
     w_copies.append(pltpu.make_async_copy(wo_hbm, wo, w_sem.at[3]))
-    for copy in w_copies:
+    x_copy = pltpu.make_async_copy(x_hbm, x_ref, w_sem.at[4])
+    ct_copy = pltpu.make_async_copy(ct_hbm, ct_ref, w_sem.at[5])
+    for copy in (x_copy, *w_copies, ct_copy):
         copy.start()
 
     barrier = pltpu.get_barrier_semaphore()
@@ -67,6 +69,7 @@
         pl.semaphore_signal(barrier, inc=1, device_id=to((me + i) % 16),
                             device_id_type=pl.DeviceIdType.MESH)
 
+    x_copy.wait()
     for n in range(rows // CHUNK):
         part = pl.ds(n * CHUNK, CHUNK)
         x = x_ref[part, :].astype(F32)
@@ -104,28 +107,25 @@
     def _():
         h_recv[1] = jnp.zeros(h_recv.shape[1:], BF16)
 
-    acts_t[0:channels, :] = acts[...].astype(F32).T.astype(BF16)
-    acts_t[channels:, :] = acts_t[0:own_rows, :]
-
-    def block_of(target):
-        return acts_t.at[pl.ds(pl.multiple_of((target * own_rows) % channels, SUB), own_rows)]
+    acts_t[...] = acts[...].astype(F32).T.astype(BF16)
+
+    def block_of(spot):
+        return acts_t.at[pl.ds(pl.multiple_of(spot * width, width), width)]
 
     a_copies = []
     for i in range(1, 8):
-        peer = base + (place + i) % 8
-        for b in range(2):
-            copy = remote(block_of((peer + 8 * b) % 16), blocks.at[place, b],
-                          as_sem.at[i, b], ar_sem.at[place, b], peer)
-            copy.start()
-            a_copies.append(copy)
-    for b in range(2):
-        blocks[place, b] = block_of((me + 8 * b) % 16)[...]
+        peer = (place + i) % 8
+        copy = remote(block_of(peer), blocks.at[place], as_sem.at[i], ar_sem.at[place], base + peer)
+        copy.start()
+        a_copies.append(copy)
+    blocks[place] = block_of(place)[...]
 
     dh[5 * half] = jnp.zeros(dh.shape[1:], BF16)
 
     w_copies[2].wait()
     h_mid = jnp.dot(acts[...], wt[channels:2 * channels, :], preferred_element_type=F32)
     w_copies[3].wait()
+    ct_copy.wait()
     back = nt_dot(ct_ref[...], wo[...])
     for n in range(rows // CHUNK):
         part = pl.ds(n * CHUNK, CHUNK)
@@ -146,39 +146,46 @@
     mine[...] = (back * slope).astype(BF16)
 
     spot = 2 * (1 + pair) + core
+    sibling = me + 1 - 2 * core
+    core_part = pl.ds(pl.multiple_of(core * rows, rows), rows)
+    edge_index = 5 * half
+    far = base + 8 - 16 * half
     d_copies = []
-    for i in (2, 6, 1, 3, 7, 5, 4):
-        peer = base + (place + i) % 8
-        copy = remote(mine, mine, ds_sem.at[i], dr_sem.at[spot], peer)
-        copy.start()
-        d_copies.append(copy)
-
-    edge_slot = 5 * half
-    far = base + 8 - 16 * half
+    for i in (1, 3, 2):
+        peer = base + 2 * ((pair + i) % 4) + core
+        d_copies.append(remote(mine, mine, ds_sem.at[i], dr_sem.at[spot], peer))
+    d_copies.append(remote(mine, mine, ds_sem.at[0], dr_sem.at[spot], sibling))
     at_edge = (me >= 6) & (me < 10)
     e_copies = [
-        remote(mine, dh.at[edge_slot, pl.ds(pl.multiple_of(core * rows, rows), rows)],
-               es_sem.at[i], dr_sem.at[2 * edge_slot + core], far + i)
-        for i in range(8)
+        remote(mine, dh.at[edge_index, core_part], es_sem.at[i],
+               dr_sem.at[2 * edge_index + core], far + 2 * i + core)
+        for i in range(4)
     ]
+    for copy in d_copies[:2]:
+        copy.start()
 
     @pl.when(at_edge)
     def _():
         for copy in e_copies:
             copy.start()
 
+    for copy in d_copies[2:]:
+        copy.start()
+
     out_ref[...] = (x_ref[...].astype(F32)
                     + jnp.dot(gated, wo[...], preferred_element_type=F32)).astype(BF16)
 
     def wait_slot(slot):
         remote(mine, mine, ds_sem.at[0], dr_sem.at[slot], mirror).wait_recv()
 
-    lower, upper = spot - 2, spot + 2
-    unused = 10 * half
-    for slot in (lower, upper):
-        @pl.when(slot // 2 != unused // 2)
-        def _(slot=slot):
-            wait_slot(slot)
+    outer = 5 - edge_index
+    f_copies = []
+    for i, index in enumerate((1 + (pair + 1) % 4, 1 + (pair + 3) % 4, outer, 1 + (pair + 2) % 4)):
+        slot = dh.at[index, core_part]
+        wait_slot(2 * index + core)
+        copy = remote(slot, slot, fs_sem.at[i], dr_sem.at[2 * index + core], sibling)
+        copy.start()
+        f_copies.append(copy)
 
     def core_rows(index):
         return dh[index, pl.ds(pl.multiple_of(core * rows, rows), rows), :]
@@ -196,30 +203,47 @@
         gi_ref[part, :] = (ct_ref[part, :].astype(F32)
                            + r_buf[part, 0:1] * (dv - first - v * second)).astype(BF16)
 
-    for slot in range(12):
-        @pl.when((slot != spot) & (slot != lower) & (slot != upper) & (slot // 2 != unused // 2))
-        def _(slot=slot):
-            wait_slot(slot)
     for i in range(1, 8):
         slot = (place + i) % 8
-        for b in range(2):
-            remote(blocks.at[slot, b], blocks.at[slot, b], as_sem.at[0, b],
-                   ar_sem.at[slot, b], mirror).wait_recv()
-
-    def term(b, j):
-        tap = (3 * ((me + 8 * b) % 16) + j) // 16
-        left = jnp.concatenate([blocks[s, b, j * SUB:(j + 1) * SUB, :] for s in range(8)], axis=1)
+        remote(blocks.at[slot], blocks.at[slot], as_sem.at[0], ar_sem.at[slot], mirror).wait_recv()
+    for i in range(4):
+        wait_slot(2 * (1 + (pair + i) % 4) + 1 - core)
+    wait_slot(2 * outer + 1 - core)
+
+    left = jnp.concatenate([blocks[i] for i in range(8)], axis=1)
+    p_copies = []
+    for n in range(3):
+        tap = (1 - half) * (2 - n) + half * n
         right = dh[pl.ds(2 - tap, 4)].reshape(8 * rows, dh.shape[2])
-        return jnp.dot(left, right, preferred_element_type=F32)
+        term = jnp.dot(left, right, preferred_element_type=F32).astype(BF16)
+        for u in range(2):
+            piece = 16 * tap + 2 * place + u
+            owner = piece // 3
+            spare = p_send.at[2 * n + u]
+            spare[...] = term[u * SUB:(u + 1) * SUB, :]
+            copy = remote(spare, p_recv.at[half, piece % 3], ps_sem.at[2 * n + u],
+                          pr_sem.at[half, piece % 3], owner)
+            p_copies.append((owner, copy))
+
+            @pl.when(owner != me)
+            def _(copy=copy):
+                copy.start()
+
+            @pl.when(owner == me)
+            def _(spare=spare, piece=piece):
+                p_recv[half, piece % 3] = spare[...]
 
     for j in range(3):
-        p_send[j * SUB:(j + 1) * SUB, :] = term(1, j).astype(BF16)
-    p_copy = remote(p_send, p_recv, ps_sem, pr_sem, mirror)
-    p_copy.start()
-    for j in range(3):
-        gt_ref[j * SUB:(j + 1) * SUB, :] = term(0, j)
-    p_copy.wait_recv()
-    gt_ref[...] = (gt_ref[...] + p_recv[...].astype(F32)) * scale
+        for h in range(2):
+            maker = 8 * h + ((3 * me + j) % 16) // 2
+
+            @pl.when(maker != me)
+            def _(h=h, j=j):
+                remote(p_send.at[0], p_recv.at[h, j], ps_sem.at[0], pr_sem.at[h, j],
+                       mirror).wait_recv()
+
+        gt_ref[j * SUB:(j + 1) * SUB, :] = (
+            p_recv[0, j].astype(F32) + p_recv[1, j].astype(F32)) * scale
 
     @pl.when(me < 14)
     def _():
@@ -234,9 +258,12 @@
         for copy in e_copies:
             copy.wait_send()
 
-    for copy in a_copies + d_copies:
+    for copy in a_copies + d_copies + f_copies:
         copy.wait_send()
-    p_copy.wait_send()
+    for owner, copy in p_copies:
+        @pl.when(owner != me)
+        def _(copy=copy):
+            copy.wait_send()
 
 
 def fused_body(inputs, cotangent, w_taps, w_out):
@@ -255,35 +282,38 @@
             jax.ShapeDtypeStruct((rows, channels), BF16),
             jax.ShapeDtypeStruct((own_rows, inner), F32),
         ),
-        in_specs=[vmem, vmem, hbm, hbm],
+        in_specs=[hbm, hbm, hbm, hbm],
         out_specs=(vmem, vmem, vmem),
         scratch_shapes=[
+            pltpu.VMEM((rows, channels), BF16),
+            pltpu.VMEM((rows, channels), BF16),
             pltpu.VMEM(w_taps.shape, BF16),
             pltpu.VMEM(w_out.shape, BF16),
             pltpu.VMEM((rows, channels), BF16),
-            pltpu.VMEM((channels + own_rows, rows), BF16),
+            pltpu.VMEM((channels, rows), BF16),
             pltpu.VMEM((rows, channels), F32),
             pltpu.VMEM((rows, channels), F32),
             pltpu.VMEM((rows, 128), F32),
-            pltpu.VMEM((8, 2, own_rows, rows), BF16),
+            pltpu.VMEM((8, channels // 8, rows), BF16),
             pltpu.VMEM((6, 2 * rows, inner), BF16),
             pltpu.VMEM((2, rows, inner), BF16),
             pltpu.VMEM((2, rows, inner), BF16),
-            pltpu.VMEM((own_rows, inner), BF16),
-            pltpu.VMEM((own_rows, inner), BF16),
-            dma((4,)),
+            pltpu.VMEM((6, SUB, inner), BF16),
+            pltpu.VMEM((2, 3, SUB, inner), BF16),
+            dma((6,)),
             dma((2,)),
             dma((2,)),
-            dma((8, 2)),
-            dma((8, 2)),
             dma((8,)),
+            dma((8,)),
+            dma((4,)),
             dma((12,)),
-            dma((8,)),
-            dma,
-            dma,
+            dma((4,)),
+            dma((4,)),
+            dma((6,)),
+            dma((2, 3)),
         ],
         compiler_params=pltpu.CompilerParams(
-            collective_id=0, has_side_effects=True, vmem_limit_bytes=48 * 1024 * 1024
+            collective_id=0, has_side_effects=True, vmem_limit_bytes=60 * 1024 * 1024
         ),
     )(inputs, cotangent, w_taps, w_out)
 

time: 58.1 us -> 42.7 us (0.73)
  the two profiles are of different devices: /device:TPU:30 before, /device:TPU:17 now
where the time goes in v2:
time: 42.7 us; the launch traced here: 42.4 us
  Pallas kernels  36.4 us (85%)
  local copies, waits for them, and re-layouts  5.34 us (13%)
  between operations  0.64 us (1%)
    pallas_call x1, Pallas kernels, fused_body(): pl.pallas_call(functools.partial(fused, scale), out_shape=(jax.ShapeDtype...  36.4 us
    unnamed x3, local copies, waits for them, and re-layouts  5.34 us

profile of v2, /device:TPU:17, one launch (start us, length us, event | category | flops | bytes accessed | tf_op | source)
XLA Modules:
  0.0 42.4 jit_solution(3376924517969282562)
XLA Ops:
  0.6 36.4 %shard_map.67 = (bf16[128,1536]{1,0:T(8,128)(2,1)}, bf16[128,1536]{1,0:T(8,128)(2,1)}, f32[288,384]{1,0:T(8,128)}) custom-call(bf16[128,1536]{1,0:T(8,128)(2,1)} %x_hbm.1, bf16[128,1536]{1,0:T(8,128)(2,1)} %ct_hbm.1, bf16[4608,384]{1,0:T(8,128)(2,1)} %wt_hbm.1, bf16[384,1536]{1,0:T(8,128)(2,1)} %wo_hbm.1), custom_call_target="tpu_custom_call" | custom-call | tf_op jit(solution)/shard_map/pallas_call | solution.py:278
  37.1 1.8 %copy.10 = bf16[128,1536]{1,0:T(8,128)(2,1)} copy(bf16[128,1536]{1,0:T(8,128)(2,1)} %get-tuple-element.6) | data formatting | bytes 786432
  38.8 1.8 %copy.11 = bf16[128,1536]{1,0:T(8,128)(2,1)} copy(bf16[128,1536]{1,0:T(8,128)(2,1)} %get-tuple-element.7) | data formatting | bytes 786432
  40.6 1.8 %copy.12 = f32[288,384]{1,0:T(8,128)} copy(f32[288,384]{1,0:T(8,128)} %get-tuple-element.8) | data formatting | bytes 884736

commit v3 on v2

--- a/solution.py
+++ b/solution.py
@@ -172,9 +172,6 @@
     for copy in d_copies[2:]:
         copy.start()
 
-    out_ref[...] = (x_ref[...].astype(F32)
-                    + jnp.dot(gated, wo[...], preferred_element_type=F32)).astype(BF16)
-
     def wait_slot(slot):
         remote(mine, mine, ds_sem.at[0], dr_sem.at[slot], mirror).wait_recv()
 
@@ -186,22 +183,6 @@
         copy = remote(slot, slot, fs_sem.at[i], dr_sem.at[2 * index + core], sibling)
         copy.start()
         f_copies.append(copy)
-
-    def core_rows(index):
-        return dh[index, pl.ds(pl.multiple_of(core * rows, rows), rows), :]
-
-    d_next, d_mid, d_prior = core_rows(pair + 2), core_rows(pair + 1), core_rows(pair)
-    d_acts = nt_dot(d_next, wt[0:channels, :])
-    d_acts = d_acts + nt_dot(d_mid, wt[channels:2 * channels, :])
-    slope_buf[...] = (d_acts + nt_dot(d_prior, wt[2 * channels:, :])) * slope_buf[...]
-    for n in range(rows // CHUNK):
-        part = pl.ds(n * CHUNK, CHUNK)
-        dv = slope_buf[part, :]
-        v = v_buf[part, :]
-        first = jnp.mean(dv, axis=1, keepdims=True)
-        second = jnp.mean(dv * v, axis=1, keepdims=True)
-        gi_ref[part, :] = (ct_ref[part, :].astype(F32)
-                           + r_buf[part, 0:1] * (dv - first - v * second)).astype(BF16)
 
     for i in range(1, 8):
         slot = (place + i) % 8
@@ -232,6 +213,25 @@
             @pl.when(owner == me)
             def _(spare=spare, piece=piece):
                 p_recv[half, piece % 3] = spare[...]
+
+    out_ref[...] = (x_ref[...].astype(F32)
+                    + jnp.dot(gated, wo[...], preferred_element_type=F32)).astype(BF16)
+
+    def core_rows(index):
+        return dh[index, pl.ds(pl.multiple_of(core * rows, rows), rows), :]
+
+    d_next, d_mid, d_prior = core_rows(pair + 2), core_rows(pair + 1), core_rows(pair)
+    d_acts = nt_dot(d_next, wt[0:channels, :])
+    d_acts = d_acts + nt_dot(d_mid, wt[channels:2 * channels, :])
+    slope_buf[...] = (d_acts + nt_dot(d_prior, wt[2 * channels:, :])) * slope_buf[...]
+    for n in range(rows // CHUNK):
+        part = pl.ds(n * CHUNK, CHUNK)
+        dv = slope_buf[part, :]
+        v = v_buf[part, :]
+        first = jnp.mean(dv, axis=1, keepdims=True)
+        second = jnp.mean(dv * v, axis=1, keepdims=True)
+        gi_ref[part, :] = (ct_ref[part, :].astype(F32)
+                           + r_buf[part, 0:1] * (dv - first - v * second)).astype(BF16)
 
     for j in range(3):
         for h in range(2):

time: 42.7 us -> 41.6 us (0.974)
  Pallas kernels: 36.4 us -> 35.4 us
    pallas_call x1, Pallas kernels: 36.4 us -> 35.4 us  [fused_body(): pl.pallas_call(functools.partial(fused, scale), out_shape=(jax.ShapeDtype...]
where the time goes in v3:
time: 41.6 us; the launch traced here: 41.4 us
  Pallas kernels  35.4 us (85%)
  local copies, waits for them, and re-layouts  5.34 us (13%)
  between operations  0.64 us (2%)
    pallas_call x1, Pallas kernels, fused_body(): pl.pallas_call(functools.partial(fused, scale), out_shape=(jax.ShapeDtype...  35.4 us
    unnamed x3, local copies, waits for them, and re-layouts  5.34 us

profile of v3, /device:TPU:17, one launch (start us, length us, event | category | flops | bytes accessed | tf_op | source)
XLA Modules:
  0.0 41.4 jit_solution(14040721032592290922)
XLA Ops:
  0.6 35.4 %shard_map.67 = (bf16[128,1536]{1,0:T(8,128)(2,1)}, bf16[128,1536]{1,0:T(8,128)(2,1)}, f32[288,384]{1,0:T(8,128)}) custom-call(bf16[128,1536]{1,0:T(8,128)(2,1)} %x_hbm.1, bf16[128,1536]{1,0:T(8,128)(2,1)} %ct_hbm.1, bf16[4608,384]{1,0:T(8,128)(2,1)} %wt_hbm.1, bf16[384,1536]{1,0:T(8,128)(2,1)} %wo_hbm.1), custom_call_target="tpu_custom_call" | custom-call | tf_op jit(solution)/shard_map/pallas_call | solution.py:278
  36.0 1.8 %copy.10 = bf16[128,1536]{1,0:T(8,128)(2,1)} copy(bf16[128,1536]{1,0:T(8,128)(2,1)} %get-tuple-element.6) | data formatting | bytes 786432
  37.8 1.8 %copy.11 = bf16[128,1536]{1,0:T(8,128)(2,1)} copy(bf16[128,1536]{1,0:T(8,128)(2,1)} %get-tuple-element.7) | data formatting | bytes 786432
  39.5 1.8 %copy.12 = f32[288,384]{1,0:T(8,128)} copy(f32[288,384]{1,0:T(8,128)} %get-tuple-element.8) | data formatting | bytes 884736
